TPU v7x, 32 devices: a whole 2x2x4 slice. The times are simulated.
32 devices in a mesh: groups: 2 (over y), blk: 4 (over z), sub: 4 (over x, core).
Axes of the slice: x: 2, y: 2, z: 4, core: 2. Of those that a mesh axis runs over, the one named last changes fastest.
Arguments:
- user_factors: float32 [256, 8192], P('sub', ('groups', 'blk')), parts along dimension 1, may hold values from -1.5 to 1.5
- item_factors: float32 [256, 8192], P('sub', ('groups', 'blk')), parts along dimension 1, may hold values from -1.5 to 1.5
- ratings: bfloat16 [4, 8192, 1024], P(None, ('groups', 'blk')), parts along dimension 1, may hold values from -6 to 6
- counts: int32 [4, 8192, 8], P(None, ('groups', 'blk')), parts along dimension 1, may hold values from 0 to 128
- occupancy: int32 [4, 64, 8], P(None, ('groups', 'blk')), parts along dimension 1, may hold values from 0 to 1
Outputs:
- users_after: float32 [256, 8192], P('sub', ('groups', 'blk')), parts along dimension 1
- items_after: float32 [256, 8192], P('sub', ('groups', 'blk')), parts along dimension 1
There are 2 independent parts, one for each index of `groups`. A program takes and returns all parts, laid end to end along the dimension named above; each array names one. Nothing has to cross between parts.
All inputs are finite; a program needn't handle non-finite values.
Results may differ from a plain program's by a relative error of at most 0.0025.
Values may be sent and summed in bfloat16 or wider, within the bound.
A program may use at most 64 MiB of HBM per device.

v0:
```python
import jax
import jax.numpy as jnp
from jax import lax
from jax.sharding import PartitionSpec as P

step_rate = 0.02


def shifted(value, axis, steps):
    count = lax.axis_size(axis)
    pairs = [(source, (source + steps) % count) for source in range(count)]
    return lax.ppermute(value, axis, pairs)


def weights_of(counts, occupied):
    row_count, tile_count = counts.shape
    lane_index = jnp.arange(128, dtype=jnp.int32)
    inside = (lane_index[None, None, :] < counts[:, :, None]).astype(jnp.float32)
    spread = jnp.broadcast_to(
        occupied[:, None, :, None].astype(jnp.float32), (row_count // 128, 128, tile_count, 128)
    )
    return inside.reshape(row_count, tile_count * 128) * spread.reshape(row_count, tile_count * 128)


def contract_first(left, right):
    return lax.dot_general(
        left, right, (((0,), (0,)), ((), ())), preferred_element_type=jnp.float32
    )


def stratum_update(user_state, item_state, low_users, low_items, scores, ratings_now, weight):
    errors = (weight * (scores - ratings_now.astype(jnp.float32))).astype(jnp.bfloat16)
    user_grad = lax.dot_general(
        low_items, errors, (((1,), (1,)), ((), ())), preferred_element_type=jnp.float32
    )
    item_grad = lax.dot_general(
        low_users, errors, (((1,), (0,)), ((), ())), preferred_element_type=jnp.float32
    )
    return (user_state - step_rate * user_grad, item_state - step_rate * item_grad)


def per_device(user_factors, item_factors, ratings, counts, occupancy):
    strata = ratings.shape[0]
    columns = user_factors.shape[0]
    user_state, item_state = (
        lax.all_gather(user_factors, "sub", axis=0, tiled=True),
        lax.all_gather(item_factors, "sub", axis=0, tiled=True),
    )
    for stratum in range(strata):
        weight = weights_of(counts[stratum], occupancy[stratum])
        low_users = user_state.astype(jnp.bfloat16)
        low_items = item_state.astype(jnp.bfloat16)
        scores = contract_first(low_users, low_items)
        user_state, item_state = stratum_update(
            user_state, item_state, low_users, low_items, scores, ratings[stratum], weight
        )
        item_state = shifted(item_state, "blk", 1)
    offset = lax.axis_index("sub") * columns
    users_after = lax.dynamic_slice_in_dim(user_state, offset, columns, 0)
    items_after = lax.dynamic_slice_in_dim(item_state, offset, columns, 0)
    return (users_after, items_after)


def solution(mesh):
    return jax.shard_map(
        per_device,
        mesh=mesh,
        in_specs=(
            P("sub", ("groups", "blk")),
            P("sub", ("groups", "blk")),
            P(None, ("groups", "blk"), None),
            P(None, ("groups", "blk"), None),
            P(None, ("groups", "blk"), None),
        ),
        out_specs=(P("sub", ("groups", "blk")), P("sub", ("groups", "blk"))),
        check_vma=False,
    )
```

profile of v0, /device:TPU:0, one launch (start us, length us, event | category | flops | bytes accessed | tf_op | source)
XLA Modules:
  0.0 191.2 jit_solution(9125837484889913255)
XLA Ops:
  7.2 0.0 all-gather.3.cloned.1.call-start
  7.2 0.7 all-gather.3.cloned.1.call-update
  7.9 0.0 all-gather.5.cloned.1.call-start
  7.9 0.7 all-gather.5.cloned.1.call-update
  8.6 0.8 slice_bitcast_fusion
  9.5 0.2 copy.7
  9.7 0.7 convert_bitcast_fusion
  10.4 18.6 %all-gather.3.cloned.1.call-done = f32[256,1024]{1,0:T(8,128)} async-done(((f32[64,1024]{1,0:T(8,128)}), f32[256,1024]{1,0:T(8,128)}) %all-gather.3.cloned.1.call-update) | async-done | bytes 1048592 | tf_op jit(solution)/shard_map/all_gather | solution.py:46
  29.0 0.0 copy-start.2
  29.0 18.3 %all-gather.5.cloned.1.call-done = f32[256,1024]{1,0:T(8,128)} async-done(((f32[64,1024]{1,0:T(8,128)}), f32[256,1024]{1,0:T(8,128)}) %all-gather.5.cloned.1.call-update) | async-done | bytes 1048592 | tf_op jit(solution)/shard_map/all_gather | solution.py:47
  47.3 0.0 copy-start.3
  47.3 1.2 lt.96
  48.6 0.3 broadcast_in_dim.8
  48.9 0.0 copy-done.2
  48.9 0.0 copy-done.3
  48.9 3.5 %fusion.7 = bf16[1024,1024]{1,0:T(8,128)(2,1)S(1)} fusion(f32[128,8,8,128]{3,2,1,0:T(8,128)S(1)} %bitcast.103, s32[128,8,8,128]{3,2,1,0:T(8,128)S(1)} %bitcast.99, bf16[4,1024,1024]{2,1,0:T(8,128)(2,1)} %param.7, s32[1024]{0:T(1024)S(1)} %iota_bitcast_fusion, f32[256,1024]{1,0:T(8,128)S(1)} %copy-done.3, f32[256,1024]{1,0:T(8,128)S(1)} %copy-done.2), kind=kOutput, calls=%fused_computation.14 | convolution fusion | flops 543686656 | bytes 14684160 | tf_op jit(solution)/shard_map/dot_general | solution.py:26
  52.4 1.8 fusion.9
  54.2 1.5 collective-permute-start
  55.7 1.0 copy.9
  56.7 0.0 copy-start.4
  56.7 2.0 %fusion.16 = f32[256,1024]{1,0:T(8,128)S(1)} fusion(f32[256,1024]{1,0:T(8,128)S(1)} %copy-done.2, bf16[1024,1024]{1,0:T(8,128)(2,1)S(1)} %fusion.7, f32[256,1024]{1,0:T(8,128)} %all-gather.5.cloned.1.call-done), kind=kOutput, calls=%fused_computation.35 | convolution fusion | flops 537657344 | bytes 5242880 | tf_op jit(solution)/shard_map/dot_general | solution.py:33
  58.7 0.0 copy-start
  58.8 22.9 %collective-permute-done = f32[256,1024]{1,0:T(8,128)} collective-permute-done((f32[256,1024]{1,0:T(8,128)}, f32[256,1024]{1,0:T(8,128)}, u32[]{:S(2)}, u32[]{:S(2)}) %collective-permute-start) | collective-permute-done | bytes 1048608 | tf_op jit(solution)/shard_map/ppermute | solution.py:12
  81.6 0.0 copy-done.4
  81.6 1.2 lt.100
  82.8 0.3 broadcast_in_dim.9
  83.2 3.9 %fusion.5 = bf16[1024,1024]{1,0:T(8,128)(2,1)S(1)} fusion(f32[128,8,8,128]{3,2,1,0:T(8,128)S(1)} %bitcast.104, s32[128,8,8,128]{3,2,1,0:T(8,128)S(1)} %bitcast.100, bf16[4,1024,1024]{2,1,0:T(8,128)(2,1)} %param.7, s32[1024]{0:T(1024)S(1)} %iota_bitcast_fusion, f32[256,1024]{1,0:T(8,128)S(1)} %fusion.16, f32[256,1024]{1,0:T(8,128)} %collective-permute-done), kind=kOutput, calls=%fused_computation.10 | convolution fusion | flops 543686656 | bytes 14684160 | tf_op jit(solution)/shard_map/dot_general | solution.py:26
  87.1 0.0 copy-done
  87.1 3.0 %fusion.13 = f32[256,1024]{1,0:T(8,128)} fusion(f32[256,1024]{1,0:T(8,128)} %collective-permute-done, bf16[1024,1024]{1,0:T(8,128)(2,1)S(1)} %fusion.5, f32[256,1024]{1,0:T(8,128)S(1)} %fusion.16), kind=kOutput, calls=%fused_computation.30 | convolution fusion | flops 537657344 | bytes 5242880 | tf_op jit(solution)/shard_map/dot_general | solution.py:36
  90.0 0.0 collective-permute-start.1
  90.1 1.0 copy.10
  91.1 0.0 copy-start.5
  91.1 2.3 %fusion.14 = f32[256,1024]{1,0:T(8,128)S(1)} fusion(f32[256,1024]{1,0:T(8,128)} %copy-done, bf16[1024,1024]{1,0:T(8,128)(2,1)S(1)} %fusion.5, f32[256,1024]{1,0:T(8,128)} %collective-permute-done), kind=kOutput, calls=%fused_computation.32 | convolution fusion | flops 537657344 | bytes 5242880 | tf_op jit(solution)/shard_map/dot_general | solution.py:33
  93.4 23.2 %collective-permute-done.1 = f32[256,1024]{1,0:T(8,128)} collective-permute-done((f32[256,1024]{1,0:T(8,128)}, f32[256,1024]{1,0:T(8,128)}, u32[]{:S(2)}, u32[]{:S(2)}) %collective-permute-start.1) | collective-permute-done | bytes 1048608 | tf_op jit(solution)/shard_map/ppermute | solution.py:12
  116.6 0.0 copy-done.5
  116.7 1.2 lt.104
  117.9 0.3 broadcast_in_dim.10
  118.2 3.8 %fusion.3 = bf16[1024,1024]{1,0:T(8,128)(2,1)S(1)} fusion(f32[128,8,8,128]{3,2,1,0:T(8,128)S(1)} %bitcast.105, s32[128,8,8,128]{3,2,1,0:T(8,128)S(1)} %bitcast.101, bf16[4,1024,1024]{2,1,0:T(8,128)(2,1)} %param.7, s32[1024]{0:T(1024)S(1)} %iota_bitcast_fusion, f32[256,1024]{1,0:T(8,128)S(1)} %fusion.14, f32[256,1024]{1,0:T(8,128)} %collective-permute-done.1), kind=kOutput, calls=%fused_computation.6 | convolution fusion | flops 543686656 | bytes 14684160 | tf_op jit(solution)/shard_map/dot_general | solution.py:26
  122.1 2.9 %fusion.11 = f32[256,1024]{1,0:T(8,128)} fusion(f32[256,1024]{1,0:T(8,128)} %collective-permute-done.1, bf16[1024,1024]{1,0:T(8,128)(2,1)S(1)} %fusion.3, f32[256,1024]{1,0:T(8,128)S(1)} %fusion.14), kind=kOutput, calls=%fused_computation.26 | convolution fusion | flops 537657344 | bytes 5242880 | tf_op jit(solution)/shard_map/dot_general | solution.py:36
  125.0 0.0 collective-permute-start.2
  125.0 1.0 copy.11
  126.0 0.0 copy-start.6
  126.0 2.0 %fusion.12 = f32[256,1024]{1,0:T(8,128)S(1)} fusion(f32[256,1024]{1,0:T(8,128)S(1)} %fusion.14, bf16[1024,1024]{1,0:T(8,128)(2,1)S(1)} %fusion.3, f32[256,1024]{1,0:T(8,128)} %collective-permute-done.1), kind=kOutput, calls=%fused_computation.28 | convolution fusion | flops 537657344 | bytes 5242880 | tf_op jit(solution)/shard_map/dot_general | solution.py:33
  128.0 0.0 copy-start.1
  128.0 22.6 %collective-permute-done.2 = f32[256,1024]{1,0:T(8,128)} collective-permute-done((f32[256,1024]{1,0:T(8,128)}, f32[256,1024]{1,0:T(8,128)}, u32[]{:S(2)}, u32[]{:S(2)}) %collective-permute-start.2) | collective-permute-done | bytes 1048608 | tf_op jit(solution)/shard_map/ppermute | solution.py:12
  150.7 0.0 copy-done.6
  150.7 1.2 lt.108
  151.9 0.3 broadcast_in_dim.11
  152.2 3.9 %fusion.1 = bf16[1024,1024]{1,0:T(8,128)(2,1)S(1)} fusion(f32[128,8,8,128]{3,2,1,0:T(8,128)S(1)} %bitcast.102, s32[128,8,8,128]{3,2,1,0:T(8,128)S(1)} %bitcast.98, bf16[4,1024,1024]{2,1,0:T(8,128)(2,1)} %param.7, s32[1024]{0:T(1024)S(1)} %iota_bitcast_fusion, f32[256,1024]{1,0:T(8,128)S(1)} %fusion.12, f32[256,1024]{1,0:T(8,128)} %collective-permute-done.2), kind=kOutput, calls=%fused_computation.2 | convolution fusion | flops 543686656 | bytes 14684160 | tf_op jit(solution)/shard_map/dot_general | solution.py:26
  156.1 0.0 copy-done.1
  156.1 2.0 %fusion.10 = f32[256,1024]{1,0:T(8,128)S(1)} fusion(f32[256,1024]{1,0:T(8,128)} %collective-permute-done.2, bf16[1024,1024]{1,0:T(8,128)(2,1)S(1)} %fusion.1, f32[256,1024]{1,0:T(8,128)S(1)} %fusion.12), kind=kOutput, calls=%fused_computation.24 | convolution fusion | flops 537657344 | bytes 5242880 | tf_op jit(solution)/shard_map/dot_general | solution.py:36
  158.1 0.1 collective-permute-start.3
  158.2 2.0 %fusion.19 = f32[256,1024]{1,0:T(8,128)S(1)} fusion(bf16[1024,1024]{1,0:T(8,128)(2,1)S(1)} %fusion.1, f32[256,1024]{1,0:T(8,128)} %collective-permute-done.2), kind=kOutput, calls=%fused_computation.40 | convolution fusion | flops 537133056 | bytes 4194304 | tf_op jit(solution)/shard_map/dot_general | solution.py:33
  160.2 1.7 dynamic-slice_subtract_fusion
  161.9 20.8 %collective-permute-done.3 = f32[256,1024]{1,0:T(8,128)} collective-permute-done((f32[256,1024]{1,0:T(8,128)S(1)}, f32[256,1024]{1,0:T(8,128)}, u32[]{:S(2)}, u32[]{:S(2)}) %collective-permute-start.3) | collective-permute-done | bytes 1048608 | tf_op jit(solution)/shard_map/ppermute | solution.py:12
  182.7 1.7 constant_dynamic-slice_fusion
  (1 shorter events, 0.0 us)
Async XLA Ops:
  7.2 21.8 %all-gather.3.cloned.1.call-start = ((), (), s32[]{:S(2)}) async-start(), calls=%async_computation | async-start | bytes 1310720 | tf_op jit(solution)/shard_map/all_gather | solution.py:46
  7.9 39.4 %all-gather.5.cloned.1.call-start = ((), (), s32[]{:S(2)}) async-start(), calls=%async_computation.1 | async-start | bytes 1310720 | tf_op jit(solution)/shard_map/all_gather | solution.py:47
  29.0 19.9 %copy-start.2 = (f32[256,1024]{1,0:T(8,128)S(1)}, f32[256,1024]{1,0:T(8,128)}, u32[]{:S(2)}) copy-start(f32[256,1024]{1,0:T(8,128)} %all-gather.3.cloned.1.call-done) | copy-start | bytes 3145732
  47.3 1.6 copy-start.3
  54.2 27.4 %collective-permute-start = (f32[256,1024]{1,0:T(8,128)}, f32[256,1024]{1,0:T(8,128)}, u32[]{:S(2)}, u32[]{:S(2)}) collective-permute-start(f32[256,1024]{1,0:T(8,128)} %fusion.9), channel_id=1, source_target_pairs={{0,4},{4,8},{8,12},{12,0},{1,5},{5,9},{9,13},{13,1},{2,6},{6,10},{... | collective-permute-start | bytes 3145736 | tf_op jit(solution)/shard_map/ppermute | solution.py:12
  56.7 24.9 %copy-start.4 = (s32[1024,8]{1,0:T(8,128)S(1)}, s32[1024,8]{1,0:T(8,128)}, u32[]{:S(2)}) copy-start(s32[1024,8]{1,0:T(8,128)} %copy.9) | copy-start | bytes 98308
  58.7 28.3 %copy-start = (f32[256,1024]{1,0:T(8,128)}, f32[256,1024]{1,0:T(8,128)S(1)}, u32[]{:S(2)}) copy-start(f32[256,1024]{1,0:T(8,128)S(1)} %fusion.16) | copy-start | bytes 3145732
  90.0 26.6 %collective-permute-start.1 = (f32[256,1024]{1,0:T(8,128)}, f32[256,1024]{1,0:T(8,128)}, u32[]{:S(2)}, u32[]{:S(2)}) collective-permute-start(f32[256,1024]{1,0:T(8,128)} %fusion.13), channel_id=1, source_target_pairs={{0,4},{4,8},{8,12},{12,0},{1,5},{5,9},{9,13},{13,1},{2,6},{6,10},{... | collective-permute-start | bytes 3145736 | tf_op jit(solution)/shard_map/ppermute | solution.py:12
  91.1 25.6 %copy-start.5 = (s32[1024,8]{1,0:T(8,128)S(1)}, s32[1024,8]{1,0:T(8,128)}, u32[]{:S(2)}) copy-start(s32[1024,8]{1,0:T(8,128)} %copy.10) | copy-start | bytes 98308
  125.0 25.7 %collective-permute-start.2 = (f32[256,1024]{1,0:T(8,128)}, f32[256,1024]{1,0:T(8,128)}, u32[]{:S(2)}, u32[]{:S(2)}) collective-permute-start(f32[256,1024]{1,0:T(8,128)} %fusion.11), channel_id=1, source_target_pairs={{0,4},{4,8},{8,12},{12,0},{1,5},{5,9},{9,13},{13,1},{2,6},{6,10},{... | collective-permute-start | bytes 3145736 | tf_op jit(solution)/shard_map/ppermute | solution.py:12
  126.0 24.7 %copy-start.6 = (s32[1024,8]{1,0:T(8,128)S(1)}, s32[1024,8]{1,0:T(8,128)}, u32[]{:S(2)}) copy-start(s32[1024,8]{1,0:T(8,128)} %copy.11) | copy-start | bytes 98308
  128.0 28.1 %copy-start.1 = (f32[256,1024]{1,0:T(8,128)}, f32[256,1024]{1,0:T(8,128)S(1)}, u32[]{:S(2)}) copy-start(f32[256,1024]{1,0:T(8,128)S(1)} %fusion.12) | copy-start | bytes 3145732
  158.1 24.6 %collective-permute-start.3 = (f32[256,1024]{1,0:T(8,128)S(1)}, f32[256,1024]{1,0:T(8,128)}, u32[]{:S(2)}, u32[]{:S(2)}) collective-permute-start(f32[256,1024]{1,0:T(8,128)S(1)} %fusion.10), channel_id=1, source_target_pairs={{0,4},{4,8},{8,12},{12,0},{1,5},{5,9},{9,13},{13,1},{2,6},{6,10},{... | collective-permute-start | bytes 3145736 | tf_op jit(solution)/shard_map/ppermute | solution.py:12
Sparse Core Ops, SparseCore 0:
  9.6 19.4 all-gather.2
  30.6 16.7 all-gather.4
where the time goes:
time: 192 us; the launch traced here: 191 us
  waiting for transfers between devices  128 us (67%)
  matrix products  33.1 us (17%)
  between operations  14.3 us (7%)
  local copies, waits for them, and re-layouts  11.9 us (6%)
  other arithmetic  2.45 us (1%)
    ppermute x4, waiting for transfers between devices, shifted(): return lax.ppermute(value, axis, pairs)  89.6 us
    all_gather x1, waiting for transfers between devices, per_device(): lax.all_gather(user_factors, 'sub', axis=0, tiled=True)  18.6 us
    all_gather x1, waiting for transfers between devices, per_device(): lax.all_gather(item_factors, 'sub', axis=0, tiled=True)  18.3 us
    dot_general x4, matrix products, contract_first(): lax.dot_general(left, right, (((0,), (0,)), ((), ())), preferred_element_...  15.1 us
    dot_general x4, matrix products, stratum_update(): lax.dot_general(low_users, errors, (((1,), (0,)), ((), ())), preferred_el...  9.64 us
    lt x10, local copies, waits for them, and re-layouts, weights_of(): lane_index[None, None, :] < counts[:, :, None]  8.9 us
    dot_general x4, matrix products, stratum_update(): lax.dot_general(low_items, errors, (((1,), (1,)), ((), ())), preferred_el...  8.38 us
  transfers between devices with their start and end apart: 6, of which 6 were waited for; matrix products, arithmetic and copies ran while one was open for 8% of the time, Pallas kernels for 0%

commit v1 on v0

v1 whole, which is shorter than its diff:
```python
import functools

import jax
import jax.numpy as jnp
from jax import lax
from jax.experimental import pallas as pl
from jax.experimental.pallas import tpu as pltpu
from jax.sharding import PartitionSpec as P

step_rate = 0.02
LO = 2
CHUNKS = 2
PARTS = 2
F32, BF16 = jnp.float32, jnp.bfloat16


def dot_nn(a, b):
    return lax.dot_general(a, b, (((1,), (0,)), ((), ())), preferred_element_type=F32)


def dot_nt(a, b):
    return lax.dot_general(a, b, (((1,), (1,)), ((), ())), preferred_element_type=F32)


def kernel(
    n_blk, n_sub, strata,
    users_ref, items_ref, counts_ref, occ_ref, ratings_ref,
    users_out, items_out,
    low_u, rest_u, low_ut, state_u, part_s, part_r, last_s, last_r,
    own_i, own_rest, slots, rests, hop_s, hop_rest, final_s, final_r, errors, rat, weight,
    rat_sem, u_s, u_r, v_s, v_r, i_s, i_r, j_s, j_r, z_s, z_r, y_s, y_r, f_s, f_r, g_s, g_r, p_s, p_r,
):
    n_hi = n_sub // LO
    rows, users = users_ref.shape
    ranks = rows * n_sub
    items = items_ref.shape[1]
    half = items // LO
    width = half // CHUNKS
    pair = LO * rows
    part = users // PARTS
    blk = lax.axis_index("blk")
    me = lax.axis_index("sub")
    hi, lo = me // LO, me % LO

    def at_blk(steps):
        return lax.rem(blk + steps % n_blk, n_blk)

    def at_hi(steps):
        return lax.rem(hi + steps, n_hi)

    def at_lo(steps):
        return lax.rem(lo + steps, LO)

    def sub_of(hi_at, lo_at):
        return hi_at * LO + lo_at

    def rows_of(sub_at):
        return pl.ds(pl.multiple_of(sub_at * rows, rows), rows)

    def pair_of(hi_at):
        return pl.ds(pl.multiple_of(hi_at * pair, pair), pair)

    def send(src, dst, send_sem, recv_sem, blk_at, sub_at):
        copy = pltpu.make_async_remote_copy(
            src_ref=src, dst_ref=dst, send_sem=send_sem, recv_sem=recv_sem,
            device_id={"blk": blk_at, "sub": sub_at}, device_id_type=pl.DeviceIdType.MESH,
        )
        copy.start()
        return copy

    def arrived(dst, recv_sem):
        pltpu.make_async_remote_copy(
            src_ref=dst, dst_ref=dst, send_sem=recv_sem, recv_sem=recv_sem,
            device_id={"blk": blk, "sub": me}, device_id_type=pl.DeviceIdType.MESH,
        ).wait_recv()

    sent = []
    loads = []
    for s in range(strata):
        load = pltpu.make_async_copy(
            ratings_ref.at[s, :, pl.ds(pl.multiple_of(lo * half, half), half)],
            rat.at[s], rat_sem.at[s],
        )
        load.start()
        loads.append(load)

    barrier = pltpu.get_barrier_semaphore()
    greeted = [(0, dh, dl) for dh in range(n_hi) for dl in range(LO) if (dh, dl) != (0, 0)]
    for d in sorted({sign * k % n_blk for k in (1,) for sign in (1, -1)} - {0}):
        greeted += [(d, 0, dl) for dl in range(LO)]
    for d, dh, dl in greeted:
        pl.semaphore_signal(
            barrier, inc=1,
            device_id={"blk": at_blk(d), "sub": sub_of(at_hi(dh), at_lo(dl))},
            device_id_type=pl.DeviceIdType.MESH,
        )

    def split(value):
        high = value.astype(BF16)
        return high, (value - high.astype(F32)).astype(BF16)

    low_u[rows_of(me), :], rest_u[rows_of(me), :] = split(users_ref[...])
    for h in range(LO):
        for k in range(CHUNKS):
            cols = slice((h * CHUNKS + k) * width, (h * CHUNKS + k + 1) * width)
            own_i[h, k], own_rest[h, k] = split(items_ref[:, cols])
    for k in range(CHUNKS):
        slots[0, k, rows_of(me), :] = own_i[lo, k]
        rests[0, k, rows_of(me), :] = own_rest[lo, k]
    pl.semaphore_wait(barrier, len(greeted))

    mine = low_u.at[rows_of(me), :]
    for dh in range(1, n_hi):
        sent.append(send(mine, mine, u_s.at[dh], u_r.at[me], blk, sub_of(at_hi(dh), lo)))
    sent.append(send(mine, mine, u_s.at[0], u_r.at[me], blk, sub_of(hi, at_lo(1))))
    user_sent = list(sent)
    sent.clear()
    for k in range(CHUNKS):
        at = 0
        for dl in range(LO):
            for dh in range(n_hi):
                if (dh, dl) == (0, 0):
                    continue
                sent.append(send(
                    own_i.at[at_lo(dl), k], slots.at[0, k, rows_of(me), :],
                    i_s.at[k, at], i_r.at[k, me], blk, sub_of(at_hi(dh), at_lo(dl)),
                ))
                at += 1
    mine = rest_u.at[rows_of(me), :]
    for dh in range(1, n_hi):
        sent.append(send(mine, mine, v_s.at[dh], v_r.at[me], blk, sub_of(at_hi(dh), lo)))
    sent.append(send(mine, mine, v_s.at[0], v_r.at[me], blk, sub_of(hi, at_lo(1))))
    for k in range(CHUNKS):
        sent.append(send(
            own_rest.at[at_lo(1), k], rests.at[0, k, rows_of(me), :],
            j_s.at[k], j_r.at[k], blk, sub_of(hi, at_lo(1)),
        ))

    tiles = counts_ref.shape[2]
    group = users // occ_ref.shape[1]
    tile_width = items // tiles
    tile_at = lax.broadcasted_iota(jnp.int32, (tiles, half), 0)
    lane_at = lax.broadcasted_iota(jnp.int32, (tiles, half), 1)
    spread = jnp.where((lane_at + lo * half) // tile_width == tile_at, 1.0, 0.0).astype(BF16)
    position = (lax.broadcasted_iota(jnp.int32, (group, half), 1) % tile_width).astype(F32)

    def make_weight(s):
        for b in range(users // group):
            seen = counts_ref[s, b * group:(b + 1) * group, :] * occ_ref[s, b:b + 1, :]
            seen = dot_nn(seen.astype(F32).astype(BF16), spread)
            weight[s, b * group:(b + 1) * group, :] = jnp.where(position < seen, 1.0, 0.0).astype(BF16)

    make_weight(0)
    for dh in range(1, n_hi):
        other = sub_of(at_hi(dh), lo)
        piece = low_u.at[rows_of(other), :]
        arrived(piece, u_r.at[other])
        user_sent.append(send(piece, piece, u_s.at[n_hi - 1 + dh], u_r.at[other], blk, sub_of(hi, at_lo(1))))
    for s in range(1, strata):
        make_weight(s)
    for dh in range(n_hi):
        other = sub_of(at_hi(dh), at_lo(1))
        arrived(low_u.at[rows_of(other), :], u_r.at[other])
    low_ut[...] = low_u[...].T

    def pass_on(s, k):
        arrived(slots.at[s, k, pair_of(hi), :], z_r.at[s, k])
        piece = slots.at[s, k, pair_of(hi), :]
        for dh in range(1, n_hi):
            sent.append(send(piece, piece, f_s.at[s, k, dh], f_r.at[s, k, hi], blk, sub_of(at_hi(dh), lo)))

    for s in range(strata):
        last = s == strata - 1
        loads[s].wait()
        for k in range(CHUNKS):
            if s == 0:
                for dh in range(n_hi):
                    for dl in range(LO):
                        if (dh, dl) != (0, 0):
                            other = sub_of(at_hi(dh), at_lo(dl))
                            arrived(slots.at[0, k, rows_of(other), :], i_r.at[k, other])
            else:
                if k > 0:
                    pass_on(s, k)
                for dh in range(1, n_hi):
                    other = at_hi(dh)
                    arrived(slots.at[s, k, pair_of(other), :], f_r.at[s, k, other])
            cols = slice(k * width, (k + 1) * width)
            scores = dot_nn(low_ut[...], slots[s, k])
            error = (scores - rat[s, :, cols].astype(F32)).astype(BF16) * weight[s, :, cols]
            errors[:, cols] = error
            step = step_rate * dot_nn(low_u[pair_of(hi), :], error)
            if s == 0:
                arrived(rests.at[0, k, rows_of(sub_of(hi, at_lo(1))), :], j_r.at[k])
            else:
                arrived(rests.at[s, k, pair_of(hi), :], y_r.at[s, k])
            after = slots[s, k, pair_of(hi), :].astype(F32) + rests[s, k, pair_of(hi), :].astype(F32) - step
            if not last:
                hop_s[s, k], hop_rest[s, k] = split(after)
                sent.append(send(
                    hop_s.at[s, k], slots.at[s + 1, k, pair_of(hi), :],
                    z_s.at[s, k], z_r.at[s + 1, k], at_blk(1), me,
                ))
            else:
                for h in range(LO):
                    final_s[k, h] = after[h * rows:(h + 1) * rows, :]
                for dl in range(LO):
                    sent.append(send(
                        final_s.at[k, at_lo(dl)], final_r.at[lo, k],
                        g_s.at[k, dl], g_r.at[lo, k], at_blk(1), sub_of(hi, at_lo(dl)),
                    ))
        if not last:
            for k in range(CHUNKS):
                sent.append(send(
                    hop_rest.at[s, k], rests.at[s + 1, k, pair_of(hi), :],
                    y_s.at[s, k], y_r.at[s + 1, k], at_blk(1), me,
                ))
        for p in range(PARTS):
            of_part = slice(p * part, (p + 1) * part)
            total = None
            for k in range(CHUNKS):
                held = slots[s, k] if not last else slots[s, k, pair_of(hi), :]
                grad = dot_nt(held, errors[of_part, k * width:(k + 1) * width])
                total = grad if total is None else total + grad
            if not last:
                part_s[s, p] = total
                sent.append(send(
                    part_s.at[s, p], part_r.at[s, p], p_s.at[s, p], p_r.at[s, p],
                    blk, sub_of(hi, at_lo(1)),
                ))
            else:
                for h in range(LO):
                    last_s[p, h] = total[h * rows:(h + 1) * rows, :]
                sent.append(send(
                    last_s.at[p, at_lo(1)], last_r.at[p], p_s.at[s, p], p_r.at[s, p],
                    blk, sub_of(hi, at_lo(1)),
                ))
        if s == 0:
            for dh in range(1, n_hi):
                other = sub_of(at_hi(dh), lo)
                piece = rest_u.at[rows_of(other), :]
                arrived(piece, v_r.at[other])
                sent.append(send(
                    piece, piece, v_s.at[n_hi - 1 + dh], v_r.at[other], blk, sub_of(hi, at_lo(1)),
                ))
            for dh in range(n_hi):
                other = sub_of(at_hi(dh), at_lo(1))
                arrived(rest_u.at[rows_of(other), :], v_r.at[other])
            for copy in user_sent:
                copy.wait_send()
        if not last:
            pass_on(s + 1, 0)
        for p in range(PARTS):
            of_part = slice(p * part, (p + 1) * part)
            if not last:
                arrived(part_r.at[s, p], p_r.at[s, p])
                before = state_u[:, of_part]
                if s == 0:
                    before = low_u[:, of_part].astype(F32) + rest_u[:, of_part].astype(F32)
                after = before - step_rate * (part_s[s, p] + part_r[s, p])
                state_u[:, of_part] = after
                after = after.astype(BF16)
                low_u[:, of_part] = after
                low_ut[of_part, :] = after.T
            else:
                arrived(last_r.at[p], p_r.at[s, p])
                users_out[:, of_part] = state_u[rows_of(me), of_part] - step_rate * (last_s[p, lo] + last_r[p])

    for dl in range(LO):
        for k in range(CHUNKS):
            arrived(final_r.at[at_lo(dl), k], g_r.at[at_lo(dl), k])
    for h in range(LO):
        for k in range(CHUNKS):
            items_out[:, (h * CHUNKS + k) * width:(h * CHUNKS + k + 1) * width] = final_r[h, k]
    for copy in sent:
        copy.wait_send()


def per_device(n_blk, n_sub, user_factors, item_factors, ratings, counts, occupancy):
    strata, users, items = ratings.shape
    rows = user_factors.shape[0]
    ranks = rows * n_sub
    half = items // LO
    width = half // CHUNKS
    pair = LO * rows
    n_hi = n_sub // LO
    part = users // PARTS
    vmem = pl.BlockSpec(memory_space=pltpu.VMEM)
    dma = pltpu.SemaphoreType.DMA
    return pl.pallas_call(
        functools.partial(kernel, n_blk, n_sub, strata),
        out_shape=(
            jax.ShapeDtypeStruct((rows, users), F32),
            jax.ShapeDtypeStruct((rows, items), F32),
        ),
        in_specs=[vmem] * 4 + [pl.BlockSpec(memory_space=pl.ANY)],
        out_specs=(vmem, vmem),
        scratch_shapes=[
            pltpu.VMEM((ranks, users), BF16),
            pltpu.VMEM((ranks, users), BF16),
            pltpu.VMEM((users, ranks), BF16),
            pltpu.VMEM((ranks, users), F32),
            pltpu.VMEM((strata - 1, PARTS, ranks, part), F32),
            pltpu.VMEM((strata - 1, PARTS, ranks, part), F32),
            pltpu.VMEM((PARTS, LO, rows, part), F32),
            pltpu.VMEM((PARTS, rows, part), F32),
            pltpu.VMEM((LO, CHUNKS, rows, width), BF16),
            pltpu.VMEM((LO, CHUNKS, rows, width), BF16),
            pltpu.VMEM((strata, CHUNKS, ranks, width), BF16),
            pltpu.VMEM((strata, CHUNKS, ranks, width), BF16),
            pltpu.VMEM((strata - 1, CHUNKS, pair, width), BF16),
            pltpu.VMEM((strata - 1, CHUNKS, pair, width), BF16),
            pltpu.VMEM((CHUNKS, LO, rows, width), F32),
            pltpu.VMEM((LO, CHUNKS, rows, width), F32),
            pltpu.VMEM((users, half), BF16),
            pltpu.VMEM((strata, users, half), BF16),
            pltpu.VMEM((strata, users, half), BF16),
            dma((strata,)),
            dma((2 * n_hi,)),
            dma((n_sub,)),
            dma((2 * n_hi,)),
            dma((n_sub,)),
            dma((CHUNKS, n_sub)),
            dma((CHUNKS, n_sub)),
            dma((CHUNKS,)),
            dma((CHUNKS,)),
            dma((strata, CHUNKS)),
            dma((strata, CHUNKS)),
            dma((strata, CHUNKS)),
            dma((strata, CHUNKS)),
            dma((strata, CHUNKS, n_hi)),
            dma((strata, CHUNKS, n_hi)),
            dma((CHUNKS, LO)),
            dma((LO, CHUNKS)),
            dma((strata, PARTS)),
            dma((strata, PARTS)),
        ],
        compiler_params=pltpu.CompilerParams(
            collective_id=0, has_side_effects=True, vmem_limit_bytes=52 * 2**20
        ),
        cost_estimate=pl.CostEstimate(
            flops=6 * strata * ranks * users * half, transcendentals=0,
            bytes_accessed=strata * users * items * 2,
        ),
    )(user_factors, item_factors, counts, occupancy, ratings)


def solution(mesh):
    return jax.shard_map(
        functools.partial(per_device, mesh.shape["blk"], mesh.shape["sub"]),
        mesh=mesh,
        in_specs=(
            P("sub", ("groups", "blk")),
            P("sub", ("groups", "blk")),
            P(None, ("groups", "blk"), None),
            P(None, ("groups", "blk"), None),
            P(None, ("groups", "blk"), None),
        ),
        out_specs=(P("sub", ("groups", "blk")), P("sub", ("groups", "blk"))),
        check_vma=False,
    )
```

time: 192 us -> 55.6 us (0.29)
  waiting for transfers between devices: 128 us -> 0 us
  Pallas kernels: 0 us -> 47.8 us
  matrix products: 33.1 us -> 0 us
  between operations: 14.3 us -> 0.64 us
  local copies, waits for them, and re-layouts: 11.9 us -> 6.87 us
  other arithmetic: 2.45 us -> 0 us
    ppermute x4 -> x0, waiting for transfers between devices: 89.6 us -> none  [shifted(): return lax.ppermute(value, axis, pairs)]
    pallas_call x0 -> x1, Pallas kernels: none -> 47.8 us  [per_device(): pl.pallas_call(functools.partial(kernel, n_blk, n_sub, strata), out_shape...]
    all_gather x2 -> x0, waiting for transfers between devices: 36.9 us -> none  [the longest x1 18.6 us: per_device(): lax.all_gather(user_factors, 'sub', axis=0, tiled=True)]
    dot_general x12 -> x0, matrix products: 33.1 us -> none  [the longest x4 15.1 us: contract_first(): lax.dot_general(left, right, (((0,), (0,)), ((), ())), preferred_element_...]
    lt x10 -> x0, local copies, waits for them, and re-layouts: 8.9 us -> none  [weights_of(): lane_index[None, None, :] < counts[:, :, None]]
    unnamed x14 -> x9, local copies, waits for them, and re-layouts: 0.03 us -> 6.87 us
  transfers between devices with their start and end apart: 6 -> 0, of which waited for: 6 -> 0; matrix products, arithmetic and copies ran while one was open for 8% -> 0% of each run, Pallas kernels for 0% -> 0%
where the time goes in v1:
time: 55.6 us; the launch traced here: 55.3 us
  Pallas kernels  47.8 us (86%)
  local copies, waits for them, and re-layouts  6.87 us (12%)
  between operations  0.64 us (1%)
    pallas_call x1, Pallas kernels, per_device(): pl.pallas_call(functools.partial(kernel, n_blk, n_sub, strata), out_shape...  47.8 us
    unnamed x9, local copies, waits for them, and re-layouts  6.87 us

profile of v1, /device:TPU:0, one launch (start us, length us, event | category | flops | bytes accessed | tf_op | source)
XLA Modules:
  0.0 55.3 jit_solution(16271187497498494093)
XLA Ops:
  0.6 2.8 %copy.7.counts_ref = s32[4,1024,8]{2,1,0:T(8,128)} copy(s32[4,1024,8]{1,2,0:T(8,128)} %param.8) | data formatting | bytes 262144 | tf_op args[3]
  3.5 0.0 copy-start
  3.5 0.9 %copy-done = f32[64,1024]{1,0:T(8,128)S(1)} copy-done((f32[64,1024]{1,0:T(8,128)S(1)}, f32[64,1024]{1,0:T(8,128)}, u32[]{:S(2)}) %copy-start) | copy-done | bytes 262168
  4.4 0.0 copy-start.1
  4.4 0.9 %copy-done.1 = f32[64,1024]{1,0:T(8,128)S(1)} copy-done((f32[64,1024]{1,0:T(8,128)S(1)}, f32[64,1024]{1,0:T(8,128)}, u32[]{:S(2)}) %copy-start.1) | copy-done | bytes 262168
  5.4 0.0 copy-start.2
  5.4 0.7 %copy-done.2 = s32[4,8,8]{2,1,0:T(8,128)S(1)} copy-done((s32[4,8,8]{2,1,0:T(8,128)S(1)}, s32[4,8,8]{2,1,0:T(8,128)}, u32[]{:S(2)}) %copy-start.2) | copy-done | bytes 1048
  6.1 47.8 %shard_map.68 = (f32[64,1024]{1,0:T(8,128)S(1)}, f32[64,1024]{1,0:T(8,128)S(1)}) custom-call(f32[64,1024]{1,0:T(8,128)S(1)} %copy-done, f32[64,1024]{1,0:T(8,128)S(1)} %copy-done.1, s32[4,1024,8]{2,1,0:T(8,128)} %copy.7.counts_ref, s32[4,8,8]{2,1,0:T(8,128)S(1)} %copy-done.2, bf16[4,1024,1024]{2,1,0:T(8,128)(2,1)} %ratings_ref.1), custom_call_target="tpu_custom_call" | custom-call | flops 3221225472 | bytes 8388608 | tf_op jit(solution)/shard_map/pallas_call | solution.py:290
  53.9 0.7 %copy.10 = f32[64,1024]{1,0:T(8,128)} copy(f32[64,1024]{1,0:T(8,128)S(1)} %get-tuple-element.4) | data formatting | bytes 524288
  54.6 0.7 %copy.11 = f32[64,1024]{1,0:T(8,128)} copy(f32[64,1024]{1,0:T(8,128)S(1)} %get-tuple-element.5) | data formatting | bytes 524288
Async XLA Ops:
  3.5 0.9 %copy-start = (f32[64,1024]{1,0:T(8,128)S(1)}, f32[64,1024]{1,0:T(8,128)}, u32[]{:S(2)}) copy-start(f32[64,1024]{1,0:T(8,128)} %users_ref.1) | copy-start | bytes 786436
  4.4 0.9 %copy-start.1 = (f32[64,1024]{1,0:T(8,128)S(1)}, f32[64,1024]{1,0:T(8,128)}, u32[]{:S(2)}) copy-start(f32[64,1024]{1,0:T(8,128)} %items_ref.1) | copy-start | bytes 786436
  5.4 0.7 %copy-start.2 = (s32[4,8,8]{2,1,0:T(8,128)S(1)}, s32[4,8,8]{2,1,0:T(8,128)}, u32[]{:S(2)}) copy-start(s32[4,8,8]{2,1,0:T(8,128)} %occ_ref.1) | copy-start | bytes 3076

commit v2 on v1

--- a/solution.py
+++ b/solution.py
@@ -10,6 +10,7 @@
 step_rate = 0.02
 LO = 2
 CHUNKS = 2
+PIECES = 1
 PARTS = 2
 F32, BF16 = jnp.float32, jnp.bfloat16
 
@@ -24,11 +25,12 @@
 
 def kernel(
     n_blk, n_sub, strata,
-    users_ref, items_ref, counts_ref, occ_ref, ratings_ref,
+    users_hbm, items_hbm, counts_hbm, occ_hbm, ratings_ref,
     users_out, items_out,
+    users_ref, items_ref, counts_ref, occ_ref,
     low_u, rest_u, low_ut, state_u, part_s, part_r, last_s, last_r,
     own_i, own_rest, slots, rests, hop_s, hop_rest, final_s, final_r, errors, rat, weight,
-    rat_sem, u_s, u_r, v_s, v_r, i_s, i_r, j_s, j_r, z_s, z_r, y_s, y_r, f_s, f_r, g_s, g_r, p_s, p_r,
+    in_sem, rat_sem, u_s, u_r, v_s, v_r, i_s, i_r, j_s, j_r, z_s, z_r, y_s, y_r, f_s, f_r, g_s, g_r, p_s, p_r,
 ):
     n_hi = n_sub // LO
     rows, users = users_ref.shape
@@ -76,6 +78,13 @@
 
     sent = []
     loads = []
+    first = []
+    for at, (source, target) in enumerate((
+        (users_hbm, users_ref), (items_hbm, items_ref), (counts_hbm, counts_ref), (occ_hbm, occ_ref),
+    )):
+        load = pltpu.make_async_copy(source, target, in_sem.at[at])
+        load.start()
+        first.append(load)
     for s in range(strata):
         load = pltpu.make_async_copy(
             ratings_ref.at[s, :, pl.ds(pl.multiple_of(lo * half, half), half)],
@@ -99,6 +108,8 @@
         high = value.astype(BF16)
         return high, (value - high.astype(F32)).astype(BF16)
 
+    for load in first:
+        load.wait()
     low_u[rows_of(me), :], rest_u[rows_of(me), :] = split(users_ref[...])
     for h in range(LO):
         for k in range(CHUNKS):
@@ -136,8 +147,8 @@
             j_s.at[k], j_r.at[k], blk, sub_of(hi, at_lo(1)),
         ))
 
-    tiles = counts_ref.shape[2]
-    group = users // occ_ref.shape[1]
+    tiles = counts_ref.shape[1]
+    group = users // occ_ref.shape[2]
     tile_width = items // tiles
     tile_at = lax.broadcasted_iota(jnp.int32, (tiles, half), 0)
     lane_at = lax.broadcasted_iota(jnp.int32, (tiles, half), 1)
@@ -146,8 +157,11 @@
 
     def make_weight(s):
         for b in range(users // group):
-            seen = counts_ref[s, b * group:(b + 1) * group, :] * occ_ref[s, b:b + 1, :]
-            seen = dot_nn(seen.astype(F32).astype(BF16), spread)
+            seen = counts_ref[s, :, b * group:(b + 1) * group].astype(F32).astype(BF16)
+            open_tiles = occ_ref[s, :, b:b + 1].astype(F32).astype(BF16)
+            seen = lax.dot_general(
+                seen, spread * open_tiles, (((0,), (0,)), ((), ())), preferred_element_type=F32
+            )
             weight[s, b * group:(b + 1) * group, :] = jnp.where(position < seen, 1.0, 0.0).astype(BF16)
 
     make_weight(0)
@@ -163,11 +177,18 @@
         arrived(low_u.at[rows_of(other), :], u_r.at[other])
     low_ut[...] = low_u[...].T
 
+    def piece_of(hi_at, q):
+        piece = pair // PIECES
+        return pl.ds(pl.multiple_of(hi_at * pair + q * piece, piece), piece)
+
     def pass_on(s, k):
-        arrived(slots.at[s, k, pair_of(hi), :], z_r.at[s, k])
-        piece = slots.at[s, k, pair_of(hi), :]
-        for dh in range(1, n_hi):
-            sent.append(send(piece, piece, f_s.at[s, k, dh], f_r.at[s, k, hi], blk, sub_of(at_hi(dh), lo)))
+        for q in range(PIECES):
+            piece = slots.at[s, k, piece_of(hi, q), :]
+            arrived(piece, z_r.at[s, k, q])
+            for dh in range(1, n_hi):
+                sent.append(send(
+                    piece, piece, f_s.at[s, k, q, dh], f_r.at[s, k, q, hi], blk, sub_of(at_hi(dh), lo),
+                ))
 
     for s in range(strata):
         last = s == strata - 1
@@ -180,11 +201,10 @@
                             other = sub_of(at_hi(dh), at_lo(dl))
                             arrived(slots.at[0, k, rows_of(other), :], i_r.at[k, other])
             else:
-                if k > 0:
-                    pass_on(s, k)
                 for dh in range(1, n_hi):
                     other = at_hi(dh)
-                    arrived(slots.at[s, k, pair_of(other), :], f_r.at[s, k, other])
+                    for q in range(PIECES):
+                        arrived(slots.at[s, k, piece_of(other, q), :], f_r.at[s, k, q, other])
             cols = slice(k * width, (k + 1) * width)
             scores = dot_nn(low_ut[...], slots[s, k])
             error = (scores - rat[s, :, cols].astype(F32)).astype(BF16) * weight[s, :, cols]
@@ -197,10 +217,11 @@
             after = slots[s, k, pair_of(hi), :].astype(F32) + rests[s, k, pair_of(hi), :].astype(F32) - step
             if not last:
                 hop_s[s, k], hop_rest[s, k] = split(after)
-                sent.append(send(
-                    hop_s.at[s, k], slots.at[s + 1, k, pair_of(hi), :],
-                    z_s.at[s, k], z_r.at[s + 1, k], at_blk(1), me,
-                ))
+                for q in range(PIECES):
+                    sent.append(send(
+                        hop_s.at[s, k, piece_of(0, q), :], slots.at[s + 1, k, piece_of(hi, q), :],
+                        z_s.at[s, k, q], z_r.at[s + 1, k, q], at_blk(1), me,
+                    ))
             else:
                 for h in range(LO):
                     final_s[k, h] = after[h * rows:(h + 1) * rows, :]
@@ -262,6 +283,8 @@
                 after = after.astype(BF16)
                 low_u[:, of_part] = after
                 low_ut[of_part, :] = after.T
+                for k in range(1 + p * (CHUNKS - 1) // PARTS, 1 + (p + 1) * (CHUNKS - 1) // PARTS):
+                    pass_on(s + 1, k)
             else:
                 arrived(last_r.at[p], p_r.at[s, p])
                 users_out[:, of_part] = state_u[rows_of(me), of_part] - step_rate * (last_s[p, lo] + last_r[p])
@@ -285,6 +308,7 @@
     pair = LO * rows
     n_hi = n_sub // LO
     part = users // PARTS
+    counts, occupancy = jnp.swapaxes(counts, 1, 2), jnp.swapaxes(occupancy, 1, 2)
     vmem = pl.BlockSpec(memory_space=pltpu.VMEM)
     dma = pltpu.SemaphoreType.DMA
     return pl.pallas_call(
@@ -293,9 +317,13 @@
             jax.ShapeDtypeStruct((rows, users), F32),
             jax.ShapeDtypeStruct((rows, items), F32),
         ),
-        in_specs=[vmem] * 4 + [pl.BlockSpec(memory_space=pl.ANY)],
+        in_specs=[pl.BlockSpec(memory_space=pltpu.HBM)] * 5,
         out_specs=(vmem, vmem),
         scratch_shapes=[
+            pltpu.VMEM(user_factors.shape, F32),
+            pltpu.VMEM(item_factors.shape, F32),
+            pltpu.VMEM(counts.shape, jnp.int32),
+            pltpu.VMEM(occupancy.shape, jnp.int32),
             pltpu.VMEM((ranks, users), BF16),
             pltpu.VMEM((ranks, users), BF16),
             pltpu.VMEM((users, ranks), BF16),
@@ -315,6 +343,7 @@
             pltpu.VMEM((users, half), BF16),
             pltpu.VMEM((strata, users, half), BF16),
             pltpu.VMEM((strata, users, half), BF16),
+            dma((4,)),
             dma((strata,)),
             dma((2 * n_hi,)),
             dma((n_sub,)),
@@ -324,12 +353,12 @@
             dma((CHUNKS, n_sub)),
             dma((CHUNKS,)),
             dma((CHUNKS,)),
+            dma((strata, CHUNKS, PIECES)),
+            dma((strata, CHUNKS, PIECES)),
             dma((strata, CHUNKS)),
             dma((strata, CHUNKS)),
-            dma((strata, CHUNKS)),
-            dma((strata, CHUNKS)),
-            dma((strata, CHUNKS, n_hi)),
-            dma((strata, CHUNKS, n_hi)),
+            dma((strata, CHUNKS, PIECES, n_hi)),
+            dma((strata, CHUNKS, PIECES, n_hi)),
             dma((CHUNKS, LO)),
             dma((LO, CHUNKS)),
             dma((strata, PARTS)),

time: 55.6 us -> 49.2 us (0.88)
  Pallas kernels: 47.8 us -> 43.3 us
  local copies, waits for them, and re-layouts: 6.87 us -> 5 us
    pallas_call x1, Pallas kernels: 47.8 us -> 43.3 us  [per_device(): pl.pallas_call(functools.partial(kernel, n_blk, n_sub, strata), out_shape...]
    unnamed x9, local copies, waits for them, and re-layouts: 6.87 us -> 5 us
where the time goes in v2:
time: 49.2 us; the launch traced here: 48.9 us
  Pallas kernels  43.3 us (88%)
  local copies, waits for them, and re-layouts  5 us (10%)
  between operations  0.64 us (1%)
    pallas_call x1, Pallas kernels, per_device(): pl.pallas_call(functools.partial(kernel, n_blk, n_sub, strata), out_shape...  43.3 us
    unnamed x9, local copies, waits for them, and re-layouts  5 us

profile of v2, /device:TPU:0, one launch (start us, length us, event | category | flops | bytes accessed | tf_op | source)
XLA Modules:
  0.0 48.9 jit_solution(16507181551813665089)
XLA Ops:
  0.6 0.8 %copy.7 = s32[4,8,8]{1,2,0:T(8,128)S(1)} copy(s32[4,8,8]{2,1,0:T(8,128)} %param.9) | data formatting | bytes 2048 | tf_op args[4]
  1.4 0.0 copy-start
  1.4 0.9 %copy-done = f32[64,1024]{1,0:T(8,128)S(1)} copy-done((f32[64,1024]{1,0:T(8,128)S(1)}, f32[64,1024]{1,0:T(8,128)}, u32[]{:S(2)}) %copy-start) | copy-done | bytes 262168
  2.4 0.0 copy-start.1
  2.4 0.9 %copy-done.1 = f32[64,1024]{1,0:T(8,128)S(1)} copy-done((f32[64,1024]{1,0:T(8,128)S(1)}, f32[64,1024]{1,0:T(8,128)}, u32[]{:S(2)}) %copy-start.1) | copy-done | bytes 262168
  3.3 0.0 copy-start.2
  3.3 0.9 %copy-done.2 = s32[4,1024,8]{1,2,0:T(8,128)S(1)} copy-done((s32[4,1024,8]{1,2,0:T(8,128)S(1)}, s32[4,1024,8]{1,2,0:T(8,128)}, u32[]{:S(2)}) %copy-start.2) | copy-done | bytes 131096
  4.2 43.3 %shard_map.68 = (f32[64,1024]{1,0:T(8,128)S(1)}, f32[64,1024]{1,0:T(8,128)S(1)}) custom-call(f32[64,1024]{1,0:T(8,128)S(1)} %copy-done, f32[64,1024]{1,0:T(8,128)S(1)} %copy-done.1, s32[4,8,1024]{2,1,0:T(8,128)S(1)} %bitcast.3, s32[4,8,8]{2,1,0:T(8,128)S(1)} %bitcast.2, bf16[4,1024,1024]{2,1,0:T(8,128)(2,1)} %ratings_ref.1), custom_call_target="tpu_custom_call" | custom-call | flops 3221225472 | bytes 8388608 | tf_op jit(solution)/shard_map/pallas_call | solution.py:314
  47.5 0.7 %copy.10 = f32[64,1024]{1,0:T(8,128)} copy(f32[64,1024]{1,0:T(8,128)S(1)} %get-tuple-element.4) | data formatting | bytes 524288
  48.2 0.7 %copy.11 = f32[64,1024]{1,0:T(8,128)} copy(f32[64,1024]{1,0:T(8,128)S(1)} %get-tuple-element.5) | data formatting | bytes 524288
Async XLA Ops:
  1.4 1.0 %copy-start = (f32[64,1024]{1,0:T(8,128)S(1)}, f32[64,1024]{1,0:T(8,128)}, u32[]{:S(2)}) copy-start(f32[64,1024]{1,0:T(8,128)} %users_hbm.1) | copy-start | bytes 786436
  2.4 0.9 %copy-start.1 = (f32[64,1024]{1,0:T(8,128)S(1)}, f32[64,1024]{1,0:T(8,128)}, u32[]{:S(2)}) copy-start(f32[64,1024]{1,0:T(8,128)} %items_hbm.1) | copy-start | bytes 786436
  3.3 0.9 %copy-start.2 = (s32[4,1024,8]{1,2,0:T(8,128)S(1)}, s32[4,1024,8]{1,2,0:T(8,128)}, u32[]{:S(2)}) copy-start(s32[4,1024,8]{1,2,0:T(8,128)} %param.8) | copy-start | bytes 393220
